TPU v7x, 1024 devices: a whole 4x4x32 slice. The times are simulated.
1024 devices in a mesh: dp: 64 (over z, core), replica: 16 (over y, x).
Axes of the slice: x: 4, y: 4, z: 32, core: 2. Of those that a mesh axis runs over, the one named last changes fastest.
Arguments:
- events: bfloat16 [262144, 512], P(('dp', 'replica')), may hold values from -24 to 24
- out_grad: bfloat16 [262144, 512], P(('dp', 'replica')), may hold values from -6 to 6
- in_proj: float32 [512, 1536], replicated, may hold values from -0.25 to 0.25
- out_proj: float32 [512, 512], replicated, may hold values from -0.25 to 0.25
- lengths: int32 [64, 16, 65], P(None, 'replica'), may hold values from 1 to 128, as said below
- offsets: int32 [64, 16, 65], P(None, 'replica'), may hold values from 0 to 254, as said below
- targets: int32 [64, 16, 65], P(None, 'replica'), may hold values from 0 to 63, as said below
Outputs:
- input_grad: float32 [262144, 512], P(('dp', 'replica'))
- packed_grad: float32 [131072, 512], P(('dp', 'replica'))
- grad_in_proj: float32 [512, 1536], P('dp')
- grad_out_proj: float32 [512, 512], P('dp')
Inputs may be any that keep to these rules, and one draw needn't show every extreme that they name: `lengths`: user 0 of every device is its long user, of 3 to 128 events; users 1 to 64 are its short users, of 1 to 2 events. In one replica index every short user has exactly 2 events. `offsets`: the long user begins at row 0; short user u begins at row 1 * 128 + 2 * k, where k runs over a permutation of 0 to 63 on each device. The long user's target is its own dp index; the 64 short users of a device have 64 different targets.
All inputs are finite; a program needn't handle non-finite values.
Results may differ from a plain program's by a relative error of at most 0.024.
Values may be sent and summed in bfloat16 or wider, within the bound.
A program may use at most 32 MiB of HBM per device.

v0:
```python
import jax
import jax.numpy as jnp
from jax import lax
from jax.sharding import PartitionSpec as P

D = 512
HEADS = 4
QK_DIM = 64
VDIM = 128
TILE = 128
CAP = 2
LONG = 1


def row_norm(values):
    centered = values - jnp.mean(values, axis=-1, keepdims=True)
    return centered / jnp.sqrt(jnp.mean(centered * centered, axis=-1, keepdims=True) + 1e-05)


def norm_cast(values):
    return row_norm(values).astype(jnp.bfloat16)


def long_layout(length, width):
    row_pos = jnp.arange(width)
    row_len = jnp.zeros((width,), jnp.int32) + length
    return (row_len, row_pos, jnp.zeros((width,), jnp.int32))


def pool_layout(slot_lengths):
    width = slot_lengths.shape[0] * CAP
    rows_idx = jnp.arange(width)
    row_seg = rows_idx // CAP
    row_pos = rows_idx % CAP
    lanes = jnp.arange(slot_lengths.shape[0])
    row_len = jnp.sum(
        jnp.where(row_seg[:, None] == lanes[None, :], slot_lengths[None, :], 0), axis=1
    )
    return (row_len, row_pos, row_seg)


def attend(projected, row_len, row_pos, row_seg):
    row_count = projected.shape[0]
    qk_width = HEADS * QK_DIM
    activated = jax.nn.silu(projected)
    gate_u = activated[:, :D]
    value_rows = activated[:, D : 2 * D].astype(jnp.bfloat16).reshape(row_count, HEADS, VDIM)
    query_rows = (
        activated[:, 2 * D : 2 * D + qk_width]
        .astype(jnp.bfloat16)
        .reshape(row_count, HEADS, QK_DIM)
    )
    key_rows = (
        activated[:, 2 * D + qk_width :].astype(jnp.bfloat16).reshape(row_count, HEADS, QK_DIM)
    )
    scores = jnp.einsum(
        "ihd,jhd->hij", query_rows, key_rows, preferred_element_type=jnp.float32
    ) * QK_DIM ** (-0.5)
    keep_pair = (
        (row_seg[None, :] == row_seg[:, None])
        & (row_pos[None, :] <= row_pos[:, None])
        & (row_pos < row_len)[:, None]
    )
    divisor = jnp.maximum(row_len, 1).astype(jnp.float32)[None, :, None]
    weights = jnp.where(keep_pair[None], jax.nn.silu(scores) / divisor, 0.0).astype(jnp.bfloat16)
    mixed_rows = jnp.einsum(
        "hij,jhd->ihd", weights, value_rows, preferred_element_type=jnp.float32
    ).reshape(row_count, D)
    return (gate_u * row_norm(mixed_rows)).astype(jnp.bfloat16)


def block_pass(rows_in, grad_block, layout, w_in, w_out):
    row_len, row_pos, row_seg = layout
    live_rows = row_pos < row_len
    grad_live = jnp.where(live_rows[:, None], grad_block, jnp.zeros_like(grad_block))
    normed, norm_back = jax.vjp(norm_cast, rows_in.astype(jnp.float32))
    projected = jnp.dot(normed, w_in, preferred_element_type=jnp.float32)
    hidden, core_back = jax.vjp(
        lambda value_in: attend(value_in, row_len, row_pos, row_seg), projected
    )
    dhidden = jnp.dot(grad_live, w_out.T, preferred_element_type=jnp.float32).astype(jnp.bfloat16)
    grad_proj = core_back(dhidden)[0].astype(jnp.bfloat16)
    dnormed = jnp.dot(grad_proj, w_in.T, preferred_element_type=jnp.float32).astype(jnp.bfloat16)
    grad_rows = norm_back(dnormed)[0] + grad_live.astype(jnp.float32)
    grad_rows = jnp.where(live_rows[:, None], grad_rows, 0.0)
    return (grad_rows, normed, grad_proj, hidden, grad_live)


def on_device(events, out_grad, in_proj, out_proj, lengths, offsets, targets):
    w_in = in_proj.astype(jnp.bfloat16)
    w_out = out_proj.astype(jnp.bfloat16)
    in_width = in_proj.shape[1]
    group_size = lax.axis_size("dp")
    my_index = lax.axis_index("dp")
    long_rows = LONG * TILE
    own_lengths = lax.dynamic_index_in_dim(lengths[:, 0, :], my_index, 0, keepdims=False)
    own_offsets = lax.dynamic_index_in_dim(offsets[:, 0, :], my_index, 0, keepdims=False)
    own_targets = lax.dynamic_index_in_dim(targets[:, 0, :], my_index, 0, keepdims=False)
    lane_ids = jnp.arange(group_size)
    slot_ids = (own_offsets[1:] - long_rows) // CAP
    target_mask = own_targets[None, 1:] == lane_ids[:, None]
    slot_of_target = jnp.sum(jnp.where(target_mask, slot_ids[None, :], 0), axis=1)
    long_pass = block_pass(
        events[:long_rows],
        out_grad[:long_rows],
        long_layout(own_lengths[0], long_rows),
        w_in,
        w_out,
    )
    pool_events = events[long_rows:].reshape(group_size, CAP, D)[slot_of_target]
    pool_grads = out_grad[long_rows:].reshape(group_size, CAP, D)[slot_of_target]
    got_events, got_grads = (
        lax.all_to_all(pool_events, "dp", split_axis=0, concat_axis=0, tiled=True),
        lax.all_to_all(pool_grads, "dp", split_axis=0, concat_axis=0, tiled=True),
    )
    source_mask = targets[:, 0, 1:] == my_index
    source_lengths = jnp.sum(jnp.where(source_mask, lengths[:, 0, 1:], 0), axis=1)
    pool_pass = block_pass(
        got_events.reshape(-1, D),
        got_grads.reshape(-1, D),
        pool_layout(source_lengths),
        w_in,
        w_out,
    )
    arrived = pool_pass[0].reshape(group_size, CAP, D)
    home_grad = jnp.concatenate(
        [long_pass[0], jnp.zeros((group_size * CAP, D), jnp.float32)], axis=0
    )
    packed = arrived.reshape(-1, D)
    normed_cols = jnp.concatenate([long_pass[1], pool_pass[1]], axis=0).T
    proj_grads = jnp.concatenate([long_pass[2], pool_pass[2]], axis=0)
    hidden_cols = jnp.concatenate([long_pass[3], pool_pass[3]], axis=0).T
    live_grads = jnp.concatenate([long_pass[4], pool_pass[4]], axis=0)
    in_term = jnp.dot(normed_cols, proj_grads, preferred_element_type=jnp.float32)
    out_term = jnp.dot(hidden_cols, live_grads, preferred_element_type=jnp.float32)
    my_rows = lax.psum_scatter(
        jnp.concatenate([in_term, out_term], axis=1), "dp", scatter_dimension=0, tiled=True
    )
    summed = lax.psum(my_rows.astype(jnp.bfloat16), "replica").astype(jnp.float32)
    return (home_grad, packed, summed[:, :in_width], summed[:, in_width:])


def solution(mesh):
    in_specs = (
        P(("dp", "replica"), None),
        P(("dp", "replica"), None),
        P(),
        P(),
        P(None, "replica", None),
        P(None, "replica", None),
        P(None, "replica", None),
    )
    out_specs = (
        P(("dp", "replica"), None),
        P(("dp", "replica"), None),
        P("dp", None),
        P("dp", None),
    )
    return jax.shard_map(
        on_device, mesh=mesh, in_specs=in_specs, out_specs=out_specs, check_vma=False
    )
```

profile of v0, /device:TPU:32, one launch (start us, length us, event | category | flops | bytes accessed | tf_op | source)
XLA Modules:
  0.0 421.3 jit_solution(12809979958357529072)
XLA Ops:
  9.2 1.5 gather_fusion
  10.6 29.0 %all-to-all-start = ((bf16[64,2,512]{2,1,0:T(2,128)(2,1)}), bf16[64,2,512]{2,1,0:T(2,128)(2,1)S(1)}, u32[]{:S(2)}, u32[]{:S(2)}) async-start(bf16[64,2,512]{2,1,0:T(2,128)(2,1)} %gather_fusion), calls=%async_computation | async-start | bytes 262144 | tf_op jit(solution)/shard_map/all_to_all | solution.py:113
  45.0 2.1 convert_element_type.176
  47.1 1.6 fusion.79
  52.8 1.4 multiply_reduce_fusion.3
  54.2 1.9 fusion.78
  56.5 1.3 fusion.31
  59.5 1.6 gather_fusion.1
  61.3 1.6 copy.64
  62.8 1.6 copy.65
  64.9 2.1 fusion.62
  67.7 1.5 fusion.12
  69.2 1.5 all-to-all-done
  70.7 20.8 %all-to-all-start.1 = ((bf16[64,2,512]{2,1,0:T(2,128)(2,1)}), bf16[64,2,512]{2,1,0:T(2,128)(2,1)S(1)}, u32[]{:S(2)}, u32[]{:S(2)}) async-start(bf16[64,2,512]{2,1,0:T(2,128)(2,1)} %gather_fusion.1), calls=%async_computation.1 | async-start | bytes 262144 | tf_op jit(solution)/shard_map/all_to_all | solution.py:114
  94.1 28.5 %all-to-all-done.1 = bf16[64,2,512]{2,1,0:T(2,128)(2,1)S(1)} async-done(((bf16[64,2,512]{2,1,0:T(2,128)(2,1)}), bf16[64,2,512]{2,1,0:T(2,128)(2,1)S(1)}, u32[]{:S(2)}, u32[]{:S(2)}) %all-to-all-start.1) | async-done | bytes 131104 | tf_op jit(solution)/shard_map/all_to_all | solution.py:114
  123.3 1.4 broadcast_select_fusion
  124.9 1.6 fusion.75
  132.9 1.5 multiply_reduce_fusion.1
  134.5 1.2 fusion.74
  136.2 1.3 fusion.34
  140.4 1.4 fusion.15
  142.5 2.2 pad_maximum_fusion
  149.6 188.5 %reduce-scatter.2.cloned.1.call-done = f32[8,2048]{1,0:T(8,128)} async-done(((f32[512,2048]{1,0:T(8,128)}), f32[8,2048]{1,0:T(8,128)}) %reduce-scatter.2.cloned.1.call-update) | async-done | bytes 65552 | tf_op jit(solution)/shard_map/reduce_scatter | solution.py:136
  338.9 74.3 %psum.7 = bf16[8,2048]{1,0:T(8,128)(2,1)S(1)} all-reduce(bf16[8,2048]{1,0:T(8,128)(2,1)S(1)} %convert_element_type.222), channel_id=1, replica_groups=mesh['dp'=64,'replica'=16] {'replica'}, use_global_device_ids=true, to_apply=%region_20.21 | all-reduce | flops 16384 | bytes 65536 | tf_op jit(solution)/shard_map/psum | solution.py:139
  (200 shorter events, 34.9 us)
Async XLA Ops:
  7.2 37.1 %copy-start.17 = (bf16[256,512]{1,0:T(8,128)(2,1)S(1)}, bf16[256,512]{1,0:T(8,128)(2,1)}, u32[]{:S(2)}) copy-start(bf16[256,512]{1,0:T(8,128)(2,1)} %param.8) | copy-start | bytes 786436
  8.2 36.1 %copy-start.35 = (s32[1024]{0:T(1024)}, s32[1024]{0:T(1024)S(1)}, u32[]{:S(2)}) copy-start(s32[1024]{0:T(1024)S(1)} %pad_clamp_fusion) | copy-start | bytes 12292
  10.6 60.1 %all-to-all-start = ((bf16[64,2,512]{2,1,0:T(2,128)(2,1)}), bf16[64,2,512]{2,1,0:T(2,128)(2,1)S(1)}, u32[]{:S(2)}, u32[]{:S(2)}) async-start(bf16[64,2,512]{2,1,0:T(2,128)(2,1)} %gather_fusion), calls=%async_computation | async-start | bytes 262144 | tf_op jit(solution)/shard_map/all_to_all | solution.py:113
  41.4 5.7 %copy-start.38 = (pred[128]{0:T(512)(128)(4,1)}, pred[128]{0:T(512)(128)(4,1)S(1)}, u32[]{:S(2)}) copy-start(pred[128]{0:T(512)(128)(4,1)S(1)} %iota_compare_fusion.3) | copy-start | bytes 388
  41.4 5.7 %copy-start.31 = (f32[128]{0:T(128)}, f32[128]{0:T(128)S(1)}, u32[]{:S(2)}) copy-start(f32[128]{0:T(128)S(1)} %broadcast_multiply_fusion.3) | copy-start | bytes 1540
  43.1 4.0 copy-start.45
  44.3 2.8 copy-start.13
  45.0 7.8 %copy-start.3 = (bf16[128,512]{1,0:T(8,128)(2,1)}, bf16[128,512]{1,0:T(8,128)(2,1)S(1)}, u32[]{:S(2)}) copy-start(bf16[128,512]{1,0:T(8,128)(2,1)S(1)} %get-tuple-element.25) | copy-start | bytes 393220
  49.6 2.4 copy-start.18
  49.7 2.8 copy-start.22
  49.7 3.0 copy-start
  56.5 3.0 copy-start.15
  56.5 11.3 %copy-start.8 = (f32[128,512]{1,0:T(8,128)S(1)}, f32[128,512]{1,0:T(8,128)}, u32[]{:S(2)}) copy-start(f32[128,512]{1,0:T(8,128)} %get-tuple-element.19) | copy-start | bytes 786436
  64.9 2.9 copy-start.51
  70.7 51.9 %all-to-all-start.1 = ((bf16[64,2,512]{2,1,0:T(2,128)(2,1)}), bf16[64,2,512]{2,1,0:T(2,128)(2,1)S(1)}, u32[]{:S(2)}, u32[]{:S(2)}) async-start(bf16[64,2,512]{2,1,0:T(2,128)(2,1)} %gather_fusion.1), calls=%async_computation.1 | async-start | bytes 262144 | tf_op jit(solution)/shard_map/all_to_all | solution.py:114
  91.5 246.6 %reduce-scatter.2.cloned.1.call-start = ((), (), s32[]{:S(2)}) async-start(), calls=%async_computation.3 | async-start | bytes 4259840 | tf_op jit(solution)/shard_map/reduce_scatter | solution.py:136
  91.8 35.7 %copy-start.55 = (f32[128]{0:T(128)}, f32[128]{0:T(128)S(1)}, u32[]{:S(2)}) copy-start(f32[128]{0:T(128)S(1)} %maximum_convert_fusion) | copy-start | bytes 1540
  93.0 33.5 %copy-start.33 = (f32[128]{0:T(128)}, f32[128]{0:T(128)S(1)}, u32[]{:S(2)}) copy-start(f32[128]{0:T(128)S(1)} %div.252) | copy-start | bytes 1540
  94.1 32.4 %copy-start.36 = (f32[128]{0:T(128)}, f32[128]{0:T(128)S(1)}, u32[]{:S(2)}) copy-start(f32[128]{0:T(128)S(1)} %sqrt.68) | copy-start | bytes 1540
  132.9 3.0 copy-start.12
  136.2 3.4 copy-start.4
  136.2 3.4 copy-start.5
  136.2 3.3 copy-start.16
  139.5 2.3 copy-start.10
  (35 other events, 43.4 us)
Sparse Core Ops, SparseCore 0:
  144.8 193.2 reduce-scatter.1
where the time goes:
time: 422 us; the launch traced here: 421 us
  waiting for transfers between devices  219 us (52%)
  blocking collectives  74.3 us (18%)
  starting transfers between devices  50 us (12%)
  other arithmetic  25.6 us (6%)
  local copies, waits for them, and re-layouts  20.2 us (5%)
  matrix products  17.7 us (4%)
  between operations  15 us (4%)
    reduce_scatter x1, waiting for transfers between devices, on_device(): lax.psum_scatter(jnp.concatenate([in_term, out_term], axis=1), 'dp', scat...  188 us
    psum x1, blocking collectives, on_device(): lax.psum(my_rows.astype(jnp.bfloat16), 'replica').astype(jnp.float32)  74.3 us
    all_to_all x1, starting transfers between devices, on_device(): lax.all_to_all(pool_events, 'dp', split_axis=0, concat_axis=0, tiled=True)  29 us
    all_to_all x1, waiting for transfers between devices, on_device(): lax.all_to_all(pool_grads, 'dp', split_axis=0, concat_axis=0, tiled=True)  28.5 us
    all_to_all x1, starting transfers between devices, on_device(): lax.all_to_all(pool_grads, 'dp', split_axis=0, concat_axis=0, tiled=True)  20.8 us
  transfers between devices with their start and end apart: 3, of which 3 were waited for; matrix products, arithmetic and copies ran while one was open for 8% of the time, Pallas kernels for 0%

commit v1 on v0

v1 whole, which is shorter than its diff:
```python
import functools

import jax
import jax.numpy as jnp
from jax import lax
from jax.experimental import pallas as pl
from jax.experimental.pallas import tpu as pltpu
from jax.sharding import PartitionSpec as P

D = 512
HEADS = 4
TILE = 128
CAP = 2
F1 = 1536
LANES = 128
SUB = 8
MESH = pl.DeviceIdType.MESH
F32 = jnp.float32
BF16 = jnp.bfloat16

NT = (((1,), (1,)), ((), ()))
TN = (((0,), (0,)), ((), ()))


def dot(a, b, dims=(((1,), (0,)), ((), ()))):
    return lax.dot_general(a, b, dims, preferred_element_type=F32)


def sigmoid(v):
    return 0.5 * jnp.tanh(0.5 * v) + 0.5


def mean_rows(v):
    return jnp.mean(v, axis=-1, keepdims=True)


def row_norm(v):
    centered = v - mean_rows(v)
    scale = lax.rsqrt(mean_rows(centered * centered) + 1e-05)
    return centered * scale, scale


def norm_back(grad, unit, scale):
    return scale * (grad - mean_rows(grad) - unit * mean_rows(grad * unit))


def compute_kernel(
    ev, og, wi, wo, ln, of, tg, home, send, parts,
    wib, wob, slope, gate, val, qry, key, wts, wslope, mixed, dproj, spread,
):
    me = lax.axis_index("dp")
    ln_row, of_row, tg_row = ln[me], of[me], tg[me]
    users = ln_row.shape[1]
    rows = lax.broadcasted_iota(jnp.int32, (TILE, 1), 0)
    lanes = lax.broadcasted_iota(jnp.int32, (1, users), 1)
    pair = lax.div(rows, CAP)
    at_slot = (of_row - TILE) == pair * CAP
    pool_len = jnp.sum(jnp.where(at_slot, ln_row, 0), axis=1, keepdims=True)
    long_len = jnp.broadcast_to(ln_row[:, 0:1], (TILE, 1))
    live_long = rows < long_len
    live_pool = lax.rem(rows, CAP) < pool_len

    for n in range(0, F1, 256):
        wib[:, n : n + 256] = wi[:, n : n + 256].astype(BF16)
    wob[...] = wo[...].astype(BF16)

    live = jnp.concatenate([live_long, live_pool], axis=0)
    unit, scale = row_norm(ev[...].astype(F32))
    normed = unit.astype(BF16)
    grad_live = jnp.where(live, og[...].astype(F32), 0.0)
    grad_b = grad_live.astype(BF16)

    for n in range(0, F1, 256):
        proj = dot(normed, wib[:, n : n + 256])
        sig = sigmoid(proj)
        act = proj * sig
        slope[:, n : n + 256] = sig + act * (1.0 - sig)
        if n < D:
            gate[:, n : n + 256] = act
        elif n < 2 * D:
            val[:, n - D : n - D + 256] = act.astype(BF16)
        elif n < 2 * D + 256:
            qry[...] = act.astype(BF16)
        else:
            key[...] = act.astype(BF16)

    cols = lax.broadcasted_iota(jnp.int32, (TILE, TILE), 1)
    row2 = lax.broadcasted_iota(jnp.int32, (TILE, TILE), 0)
    low = lax.broadcasted_iota(jnp.int32, (TILE, LANES), 1) < 64
    zero_b = jnp.zeros((TILE, LANES), BF16)
    for b in range(2):
        top = b * TILE
        keep = cols <= row2
        if b == 0:
            keep = keep & live_long
            size = long_len
        else:
            keep = keep & (lax.div(cols, CAP) == lax.div(row2, CAP)) & live_pool
            size = pool_len
        inv = 1.0 / jnp.maximum(size, 1).astype(F32)
        for h in range(HEADS):
            lane = (h // 2) * LANES
            mine = low if h % 2 == 0 else ~low
            qh = jnp.where(mine, qry[top : top + TILE, lane : lane + LANES], zero_b)
            score = dot(qh, key[top : top + TILE, lane : lane + LANES], NT) * 0.125
            sig = sigmoid(score)
            act = score * sig
            w = jnp.where(keep, act * inv, 0.0).astype(BF16)
            wts[b * HEADS + h] = w
            wslope[b * HEADS + h] = jnp.where(
                keep, (sig + act * (1.0 - sig)) * (inv * 0.125), 0.0
            )
            mixed[top : top + TILE, h * LANES : (h + 1) * LANES] = dot(
                w, val[top : top + TILE, h * LANES : (h + 1) * LANES]
            )

    unit_m, scale_m = row_norm(mixed[...])
    gate_u = gate[...]
    hidden = (gate_u * unit_m).astype(BF16)
    dhid = dot(grad_b, wob[...], NT).astype(BF16).astype(F32)
    dproj[:, :D] = (dhid * unit_m * slope[:, :D]).astype(BF16)
    dmix = norm_back(dhid * gate_u, unit_m, scale_m).astype(BF16)

    def emit(result, first):
        groups = result.shape[0] // (2 * SUB)
        for i in range(result.shape[1] // LANES):
            piece = result[:, i * LANES : (i + 1) * LANES].reshape(
                groups, 2, SUB, LANES
            )
            for c in range(2):
                parts[c, first + i] = (
                    piece[:, c].reshape(groups * SUB, LANES).astype(BF16)
                )

    hidden_t = hidden.T
    for n in range(0, D, 256):
        emit(dot(hidden_t, grad_b[:, n : n + 256]), (F1 + n) // LANES)

    for b in range(2):
        top = b * TILE
        for p in range(HEADS // 2):
            lane = p * LANES
            kk = key[top : top + TILE, lane : lane + LANES]
            qq = qry[top : top + TILE, lane : lane + LANES]
            dq, dk = [], []
            for h in (2 * p, 2 * p + 1):
                dm = dmix[top : top + TILE, h * LANES : (h + 1) * LANES]
                vh = val[top : top + TILE, h * LANES : (h + 1) * LANES]
                w = wts[b * HEADS + h]
                dw = dot(dm, vh, NT).astype(BF16).astype(F32)
                dv = dot(w, dm, TN).astype(BF16).astype(F32)
                at = D + h * LANES
                dproj[top : top + TILE, at : at + LANES] = (
                    dv * slope[top : top + TILE, at : at + LANES]
                ).astype(BF16)
                ds = (dw * wslope[b * HEADS + h]).astype(BF16)
                dq.append(dot(ds, kk))
                dk.append(dot(ds, qq, TN))
            for at, pieces in ((2 * D + lane, dq), (2 * D + 256 + lane, dk)):
                both = jnp.where(low, pieces[0], pieces[1]).astype(BF16).astype(F32)
                dproj[top : top + TILE, at : at + LANES] = (
                    both * slope[top : top + TILE, at : at + LANES]
                ).astype(BF16)

    normed_t = normed.T
    for n in range(0, F1, 256):
        emit(dot(normed_t, dproj[:, n : n + 256]), n // LANES)

    dnormed = dot(dproj[...], wib[...], NT).astype(BF16).astype(F32)
    grad = norm_back(dnormed, unit, scale) + grad_live
    grad = jnp.where(live, grad, 0.0)
    home[:TILE] = grad[:TILE]
    home[TILE:] = jnp.zeros((TILE, D), F32)

    to_target = ((tg_row == pair) & (lanes >= 1)).astype(F32).astype(BF16)
    from_slot = at_slot.astype(F32).astype(BF16)
    moves = dot(to_target, from_slot, NT)
    moves = jnp.where(lax.rem(cols, CAP) == lax.rem(row2, CAP), moves, 0.0)
    packed = dot(moves.astype(BF16), grad[TILE:].astype(BF16))
    for i in range(D // LANES):
        spread[pl.ds(i, TILE, stride=D // LANES), :] = packed[
            :, i * LANES : (i + 1) * LANES
        ]
    send[...] = spread[...].reshape(send.shape).astype(BF16)


def comm_kernel(
    n_dp, n_rep, send, parts, packed, grads,
    got, core_in, chip, rep_in, acc, z_out, z_in, fin, fin_in, spread,
    pk_s, pk_r, c_s, c_r, r_s, r_r, z_s, z_r, f_s, f_r,
):
    me = lax.axis_index("dp")
    rep = lax.axis_index("replica")
    nz = n_dp // 2
    core = lax.rem(me, 2)
    z = lax.div(me, 2)
    other = me + 1 - 2 * core

    barrier = pltpu.get_barrier_semaphore()

    def dp_peer(k):
        return lax.rem(me + k, n_dp)

    def rep_peer(k):
        return lax.rem(rep + k, n_rep)

    def z_peer(k):
        return lax.rem(z + k, nz)

    @pl.loop(1, n_dp)
    def _(k):
        pl.semaphore_signal(
            barrier, inc=1, device_id=(dp_peer(k), rep), device_id_type=MESH
        )

    @pl.loop(1, n_rep)
    def _(k):
        pl.semaphore_signal(
            barrier, inc=1, device_id=(me, rep_peer(k)), device_id_type=MESH
        )

    pl.semaphore_wait(barrier, n_dp - 1 + n_rep - 1)

    def core_copy(r):
        return pltpu.make_async_remote_copy(
            src_ref=parts.at[1 - core, r],
            dst_ref=core_in.at[r],
            send_sem=c_s.at[r],
            recv_sem=c_r.at[r],
            device_id=(other, rep),
            device_id_type=MESH,
        )

    def rep_copy(r, slot):
        return pltpu.make_async_remote_copy(
            src_ref=chip.at[r],
            dst_ref=rep_in.at[slot],
            send_sem=r_s.at[r],
            recv_sem=r_r.at[slot],
            device_id=(me, r),
            device_id_type=MESH,
        )

    def packed_copy(t):
        return pltpu.make_async_remote_copy(
            src_ref=send.at[t],
            dst_ref=got.at[me],
            send_sem=pk_s,
            recv_sem=pk_r,
            device_id=(t, rep),
            device_id_type=MESH,
        )

    def z_copy(t):
        return pltpu.make_async_remote_copy(
            src_ref=z_out.at[t],
            dst_ref=z_in.at[z],
            send_sem=z_s,
            recv_sem=z_r,
            device_id=(t * 2 + core, rep),
            device_id_type=MESH,
        )

    def fin_copy(r):
        return pltpu.make_async_remote_copy(
            src_ref=fin,
            dst_ref=fin_in.at[rep],
            send_sem=f_s.at[r],
            recv_sem=f_r,
            device_id=(me, r),
            device_id_type=MESH,
        )

    def wait_all(ref, count, sem):
        part = ref.at[pl.ds(0, count)]
        pltpu.make_async_copy(part, part, sem).wait()

    @pl.loop(1, n_rep + 1)
    def _(k):
        core_copy(rep_peer(k)).start()

    @pl.loop(1, n_dp)
    def _(k):
        packed_copy(dp_peer(k)).start()

    got[me] = send[me]

    @pl.loop(1, n_rep)
    def _(k):
        r = rep_peer(k)
        core_copy(r).wait_recv()
        chip[r] = (parts[core, r].astype(F32) + core_in[r].astype(F32)).astype(BF16)
        rep_copy(r, rep).start()

    core_copy(rep).wait_recv()
    acc[...] = parts[core, rep].astype(F32) + core_in[rep].astype(F32)

    @pl.loop(1, n_rep)
    def _(k):
        r = rep_peer(n_rep - k)
        rep_copy(r, r).wait_recv()
        acc[...] += rep_in[r].astype(F32)

    z_out[...] = acc[...].reshape(z_out.shape).astype(BF16)

    @pl.loop(1, nz)
    def _(k):
        z_copy(z_peer(k)).start()

    z_in[z] = z_out[z]
    wait_all(z_in, nz - 1, z_r)
    fin[...] = jnp.sum(z_in[...].astype(F32), axis=0)

    @pl.loop(1, n_rep)
    def _(k):
        fin_copy(rep_peer(k)).start()

    fin_in[rep] = fin[...]

    wait_all(got, n_dp - 1, pk_r)
    spread[...] = got[...].astype(F32).reshape(spread.shape)
    for i in range(D // LANES):
        packed[:, i * LANES : (i + 1) * LANES] = spread[
            pl.ds(i, packed.shape[0], stride=D // LANES), :
        ]

    wait_all(fin_in, n_rep - 1, f_r)
    for r in range(n_rep):
        grads[:, r * LANES : (r + 1) * LANES] = fin_in[r]

    @pl.loop(1, n_rep + 1)
    def _(k):
        core_copy(rep_peer(k)).wait_send()

    @pl.loop(1, n_rep)
    def _(k):
        rep_copy(rep_peer(k), rep).wait_send()
        fin_copy(rep_peer(k)).wait_send()

    wait_all(send, n_dp - 1, pk_s)
    wait_all(z_out, nz - 1, z_s)


def vmem():
    return pl.BlockSpec(memory_space=pltpu.VMEM)


def compute(events, out_grad, in_proj, out_proj, lengths, offsets, targets, n_dp, n_rep):
    rows = events.shape[0]
    half = D // 2
    return pl.pallas_call(
        compute_kernel,
        out_shape=(
            jax.ShapeDtypeStruct((rows, D), F32),
            jax.ShapeDtypeStruct((n_dp, SUB, LANES), BF16),
            jax.ShapeDtypeStruct((2, (F1 + D) // LANES, half, LANES), BF16),
        ),
        in_specs=[vmem()] * 7,
        out_specs=(vmem(), vmem(), vmem()),
        scratch_shapes=[
            pltpu.VMEM((D, F1), BF16),
            pltpu.VMEM((D, D), BF16),
            pltpu.VMEM((rows, F1), F32),
            pltpu.VMEM((rows, D), F32),
            pltpu.VMEM((rows, D), BF16),
            pltpu.VMEM((rows, 256), BF16),
            pltpu.VMEM((rows, 256), BF16),
            pltpu.VMEM((2 * HEADS, TILE, TILE), BF16),
            pltpu.VMEM((2 * HEADS, TILE, TILE), F32),
            pltpu.VMEM((rows, D), F32),
            pltpu.VMEM((rows, F1), BF16),
            pltpu.VMEM((TILE * D // LANES, LANES), F32),
        ],
        compiler_params=pltpu.CompilerParams(vmem_limit_bytes=48 * 2**20),
        name="rows",
    )(events, out_grad, in_proj, out_proj, lengths, offsets, targets)


def exchange(send, parts, n_dp, n_rep):
    nz = n_dp // 2
    deep = parts.shape[2]
    dma = pltpu.SemaphoreType.DMA
    return pl.pallas_call(
        functools.partial(comm_kernel, n_dp, n_rep),
        out_shape=(
            jax.ShapeDtypeStruct((n_dp * CAP, D), F32),
            jax.ShapeDtypeStruct((SUB, n_rep * LANES), F32),
        ),
        in_specs=[vmem()] * 2,
        out_specs=(vmem(), vmem()),
        scratch_shapes=[
            pltpu.VMEM((n_dp, SUB, LANES), BF16),
            pltpu.VMEM((n_rep, deep, LANES), BF16),
            pltpu.VMEM((n_rep, deep, LANES), BF16),
            pltpu.VMEM((n_rep, deep, LANES), BF16),
            pltpu.VMEM((deep, LANES), F32),
            pltpu.VMEM((nz, SUB, LANES), BF16),
            pltpu.VMEM((nz, SUB, LANES), BF16),
            pltpu.VMEM((SUB, LANES), F32),
            pltpu.VMEM((n_rep, SUB, LANES), F32),
            pltpu.VMEM((n_dp * SUB, LANES), F32),
            dma, dma,
            dma((n_rep,)), dma((n_rep,)),
            dma((n_rep,)), dma((n_rep,)),
            dma, dma,
            dma((n_rep,)), dma,
        ],
        compiler_params=pltpu.CompilerParams(
            collective_id=0, has_side_effects=True, vmem_limit_bytes=32 * 2**20
        ),
        name="exchange",
    )(send, parts)


def on_device(n_dp, n_rep, *args):
    home, send, parts = compute(*args, n_dp, n_rep)
    packed, grads = exchange(send, parts, n_dp, n_rep)
    return home, packed, grads[:, :F1], grads[:, F1:]


def solution(mesh):
    in_specs = (
        P(("dp", "replica"), None),
        P(("dp", "replica"), None),
        P(),
        P(),
        P(None, "replica", None),
        P(None, "replica", None),
        P(None, "replica", None),
    )
    out_specs = (
        P(("dp", "replica"), None),
        P(("dp", "replica"), None),
        P("dp", None),
        P("dp", None),
    )
    return jax.shard_map(
        functools.partial(on_device, mesh.shape["dp"], mesh.shape["replica"]),
        mesh=mesh,
        in_specs=in_specs,
        out_specs=out_specs,
        check_vma=False,
    )
```

time: 422 us -> 80.9 us (0.19)
  the two profiles are of different devices: /device:TPU:32 before, /device:TPU:4 now
where the time goes in v1:
time: 80.9 us; the launch traced here: 80.4 us
  Pallas kernels  72.4 us (89%)
  local copies, waits for them, and re-layouts  7.32 us (9%)
    pallas_call x1, Pallas kernels, exchange(): pl.pallas_call(functools.partial(comm_kernel, n_dp, n_rep), out_shape=(ja...  64.5 us
    pallas_call x1, Pallas kernels, compute(): pl.pallas_call(compute_kernel, out_shape=(jax.ShapeDtypeStruct((rows, D),...  7.9 us
    unnamed x13, local copies, waits for them, and re-layouts  6.09 us

profile of v1, /device:TPU:4, one launch (start us, length us, event | category | flops | bytes accessed | tf_op | source)
XLA Modules:
  0.0 80.4 jit_solution(13539550294915188071)
XLA Ops:
  0.6 0.0 copy-start
  0.6 1.2 %copy-done = f32[512,512]{1,0:T(8,128)S(1)} copy-done((f32[512,512]{1,0:T(8,128)S(1)}, f32[512,512]{1,0:T(8,128)}, u32[]{:S(2)}) %copy-start) | copy-done | bytes 1048600
  1.9 0.0 copy-start.1
  1.9 0.9 %copy-done.1 = bf16[256,512]{1,0:T(8,128)(2,1)S(1)} copy-done((bf16[256,512]{1,0:T(8,128)(2,1)S(1)}, bf16[256,512]{1,0:T(8,128)(2,1)}, u32[]{:S(2)}) %copy-start.1) | copy-done | bytes 262168
  2.8 0.0 copy-start.2
  2.8 0.9 %copy-done.2 = bf16[256,512]{1,0:T(8,128)(2,1)S(1)} copy-done((bf16[256,512]{1,0:T(8,128)(2,1)S(1)}, bf16[256,512]{1,0:T(8,128)(2,1)}, u32[]{:S(2)}) %copy-start.2) | copy-done | bytes 262168
  3.8 0.0 copy-start.3
  3.8 0.8 copy-done.3
  4.5 0.0 copy-start.4
  4.5 0.8 copy-done.4
  5.3 0.0 copy-start.5
  5.3 0.8 copy-done.5
  6.0 7.9 %rows.1 = (f32[256,512]{1,0:T(8,128)}, bf16[64,8,128]{2,1,0:T(8,128)(2,1)S(1)}, bf16[2,16,256,128]{3,2,1,0:T(8,128)(2,1)S(1)}) custom-call(bf16[256,512]{1,0:T(8,128)(2,1)S(1)} %copy-done.1, bf16[256,512]{1,0:T(8,128)(2,1)S(1)} %copy-done.2, f32[512,1536]{1,0:T(8,128)} %wi.1, f32[512,512]{1,0:T(8,128)S(1)} %copy-done, s32[64,1,65]{2,1,0:T(1,128)S(1)} %copy-done.3, ...), custom_call_target="tpu_custom_call" | custom-call | tf_op jit(solution)/shard_map/rows/pallas_call | solution.py:351
  13.9 64.5 %exchange.1 = (f32[128,512]{1,0:T(8,128)S(1)}, f32[8,2048]{1,0:T(8,128)S(1)}) custom-call(bf16[64,8,128]{2,1,0:T(8,128)(2,1)S(1)} %get-tuple-element.10.send, bf16[2,16,256,128]{3,2,1,0:T(8,128)(2,1)S(1)} %get-tuple-element.11.parts), custom_call_target="tpu_custom_call" | custom-call | tf_op jit(solution)/shard_map/exchange/pallas_call | solution.py:383
  78.5 0.6 slice.7
  79.1 0.6 slice.6
  79.7 0.7 copy.12
Async XLA Ops:
  0.6 1.2 %copy-start = (f32[512,512]{1,0:T(8,128)S(1)}, f32[512,512]{1,0:T(8,128)}, u32[]{:S(2)}) copy-start(f32[512,512]{1,0:T(8,128)} %wo.1) | copy-start | bytes 3145732
  1.9 0.9 %copy-start.1 = (bf16[256,512]{1,0:T(8,128)(2,1)S(1)}, bf16[256,512]{1,0:T(8,128)(2,1)}, u32[]{:S(2)}) copy-start(bf16[256,512]{1,0:T(8,128)(2,1)} %ev.1) | copy-start | bytes 786436
  2.8 0.9 %copy-start.2 = (bf16[256,512]{1,0:T(8,128)(2,1)S(1)}, bf16[256,512]{1,0:T(8,128)(2,1)}, u32[]{:S(2)}) copy-start(bf16[256,512]{1,0:T(8,128)(2,1)} %og.1) | copy-start | bytes 786436
  3.8 0.8 copy-start.3
  4.5 0.8 copy-start.4
  5.3 0.8 copy-start.5

commit v2 on v1

v2 whole, which is shorter than its diff:
```python
import functools

import jax
import jax.numpy as jnp
from jax import lax
from jax.experimental import pallas as pl
from jax.experimental.pallas import tpu as pltpu
from jax.sharding import PartitionSpec as P

D = 512
HEADS = 4
TILE = 128
CAP = 2
F1 = 1536
LANES = 128
SUB = 8
MESH = pl.DeviceIdType.MESH
F32 = jnp.float32
BF16 = jnp.bfloat16

NT = (((1,), (1,)), ((), ()))
TN = (((0,), (0,)), ((), ()))


def dot(a, b, dims=(((1,), (0,)), ((), ()))):
    return lax.dot_general(a, b, dims, preferred_element_type=F32)


def sigmoid(v):
    return 0.5 * jnp.tanh(0.5 * v) + 0.5


def mean_rows(v):
    return jnp.mean(v, axis=-1, keepdims=True)


def row_norm(v):
    centered = v - mean_rows(v)
    scale = lax.rsqrt(mean_rows(centered * centered) + 1e-05)
    return centered * scale, scale


def norm_back(grad, unit, scale):
    return scale * (grad - mean_rows(grad) - unit * mean_rows(grad * unit))


def fused_kernel(
    n_dp, nx, ny, ev_h, og_h, wi_h, wo_h, ln_h, of_h, tg_h, home, packed, grad_in, grad_out,
    ev, og, wi, wo, ln, of, tg, wib, wob, slope, gate, val, qry, key, wts, wslope, mixed,
    dproj, spread, send, got, parts, core_in, chip, one_in, mid, two_in, z_out, z_in,
    fin_out, fin_in, ld, pk_s, pk_r, c_s, c_r, o_s, o_r, t_s, t_r, z_s, z_r, f_s, f_r,
):
    me = lax.axis_index("dp")
    rep = lax.axis_index("replica")
    nz = n_dp // 2
    n_rep = nx * ny
    core = lax.rem(me, 2)
    z = lax.div(me, 2)
    a = lax.rem(rep, nx)
    b = lax.div(rep, nx)
    other = me + 1 - 2 * core
    holder = lax.rem(z, ny) == b

    def load(i, source, target):
        return pltpu.make_async_copy(source, target, ld.at[i])

    def load_w(n):
        cut = pl.ds(n * D, D)
        return load(2 + n, wi_h.at[:, cut], wi.at[:, cut])

    loads = {
        "ev": load(0, ev_h, ev), "wi0": load_w(0), "wi1": load_w(1), "wi2": load_w(2),
        "ln": load(5, ln_h, ln), "of": load(6, of_h, of), "tg": load(7, tg_h, tg),
        "og": load(1, og_h, og), "wo": load(8, wo_h, wo),
    }
    for copy in loads.values():
        copy.start()

    barrier = pltpu.get_barrier_semaphore()

    @pl.loop(1, n_dp)
    def _(k):
        pl.semaphore_signal(
            barrier, inc=1, device_id=(lax.rem(me + k, n_dp), rep), device_id_type=MESH
        )

    @pl.loop(1, n_rep)
    def _(k):
        pl.semaphore_signal(
            barrier, inc=1, device_id=(me, lax.rem(rep + k, n_rep)), device_id_type=MESH
        )

    def remote(source, target, send_sem, recv_sem, dp, replica):
        return pltpu.make_async_remote_copy(
            src_ref=source, dst_ref=target, send_sem=send_sem, recv_sem=recv_sem,
            device_id=(dp, replica), device_id_type=MESH,
        )

    def wait_all(ref, count, sem):
        part = ref.at[pl.ds(0, count)]
        pltpu.make_async_copy(part, part, sem).wait()

    def core_copy(s):
        return remote(parts.at[1 - core, s], core_in.at[s], c_s.at[s], c_r.at[s], other, rep)

    def line(s, first):
        along_x = (s % 2 == 0) == first
        return (a, nx, lambda q: b * nx + q) if along_x else (b, ny, lambda q: q * nx + a)

    def one_copies(s):
        own, count, rank = line(s, True)
        for k in range(1, count):
            peer = lax.rem(own + k, count)
            block = chip.at[s, :, peer] if s % 2 == 0 else chip.at[s, peer]
            yield peer, lambda slot, block=block, peer=peer: remote(
                block, one_in.at[s, slot], o_s.at[s, peer], o_r.at[s, slot], me, rank(peer)
            )

    def two_copies(s):
        own, count, rank = line(s, False)
        for k in range(1, count):
            peer = lax.rem(own + k, count)
            yield peer, lambda slot, peer=peer: remote(
                mid.at[s, peer], two_in.at[s, slot], t_s.at[s, peer], t_r.at[s, slot],
                me, rank(peer),
            )

    def core_step(s):
        core_copy(s).wait_recv()
        for i in range(ny):
            chip[s, i] = (
                parts[core, s, i].astype(F32) + core_in[s, i].astype(F32)
            ).astype(BF16)
        own = line(s, True)[0]
        for _, copy in one_copies(s):
            copy(own).start()

    def one_step(s):
        own = line(s, True)[0]
        peers = list(one_copies(s))
        for peer, copy in peers:
            copy(peer).wait_recv()
        block = chip[s, :, own] if s % 2 == 0 else chip[s, own]
        total = block.astype(F32)
        for peer, _ in peers:
            total = total + one_in[s, peer].astype(F32)
        mid[s] = total.astype(BF16)
        own = line(s, False)[0]
        for _, copy in two_copies(s):
            copy(own).start()

    def two_step(s):
        own = line(s, False)[0]
        peers = list(two_copies(s))
        for peer, copy in peers:
            copy(peer).wait_recv()
        total = mid[s, own].astype(F32)
        for peer, _ in peers:
            total = total + two_in[s, peer].astype(F32)
        z_out[:, s] = total.reshape(nz // ny, SUB, LANES).astype(BF16)

    rows = lax.broadcasted_iota(jnp.int32, (TILE, 1), 0)
    cols = lax.broadcasted_iota(jnp.int32, (TILE, TILE), 1)
    row2 = lax.broadcasted_iota(jnp.int32, (TILE, TILE), 0)
    low = lax.broadcasted_iota(jnp.int32, (TILE, LANES), 1) < 64
    zero_b = jnp.zeros((TILE, LANES), BF16)
    pair = lax.div(rows, CAP)

    home[TILE:] = jnp.zeros((TILE, D), F32)

    loads["ev"].wait()
    unit, scale = row_norm(ev[...].astype(F32))
    normed = unit.astype(BF16)

    for n in range(0, F1, 256):
        if n % D == 0:
            loads["wi%d" % (n // D)].wait()
        wib[:, n : n + 256] = wi[:, n : n + 256].astype(BF16)
        proj = dot(normed, wib[:, n : n + 256])
        sig = sigmoid(proj)
        act = proj * sig
        slope[:, n : n + 256] = sig + act * (1.0 - sig)
        if n < D:
            gate[:, n : n + 256] = act
        elif n < 2 * D:
            val[:, n - D : n - D + 256] = act.astype(BF16)
        elif n < 2 * D + 256:
            qry[...] = act.astype(BF16)
        else:
            key[...] = act.astype(BF16)

    for name in ("ln", "of", "tg"):
        loads[name].wait()
    ln_row, of_row, tg_row = ln[me], of[me], tg[me]
    users = ln_row.shape[1]
    lanes = lax.broadcasted_iota(jnp.int32, (1, users), 1)
    at_slot = (of_row - TILE) == pair * CAP
    pool_len = jnp.sum(jnp.where(at_slot, ln_row, 0), axis=1, keepdims=True)
    long_len = jnp.broadcast_to(ln_row[:, 0:1], (TILE, 1))
    live_long = rows < long_len
    live_pool = lax.rem(rows, CAP) < pool_len
    live = jnp.concatenate([live_long, live_pool], axis=0)

    for blk in range(2):
        top = blk * TILE
        keep = cols <= row2
        if blk == 0:
            keep = keep & live_long
            size = long_len
        else:
            keep = keep & (lax.div(cols, CAP) == lax.div(row2, CAP)) & live_pool
            size = pool_len
        inv = 1.0 / jnp.maximum(size, 1).astype(F32)
        for h in range(HEADS):
            lane = (h // 2) * LANES
            mine = low if h % 2 == 0 else ~low
            qh = jnp.where(mine, qry[top : top + TILE, lane : lane + LANES], zero_b)
            score = dot(qh, key[top : top + TILE, lane : lane + LANES], NT) * 0.125
            sig = sigmoid(score)
            act = score * sig
            w = jnp.where(keep, act * inv, 0.0).astype(BF16)
            wts[blk * HEADS + h] = w
            wslope[blk * HEADS + h] = jnp.where(
                keep, (sig + act * (1.0 - sig)) * (inv * 0.125), 0.0
            )
            mixed[top : top + TILE, h * LANES : (h + 1) * LANES] = dot(
                w, val[top : top + TILE, h * LANES : (h + 1) * LANES]
            )

    unit_m, scale_m = row_norm(mixed[...])
    hidden = (gate[...] * unit_m).astype(BF16)
    loads["og"].wait()
    grad_live = jnp.where(live, og[...].astype(F32), 0.0)
    grad_b = grad_live.astype(BF16)

    def emit(s, result, first):
        for i in range(result.shape[1] // LANES):
            piece = result[:, i * LANES : (i + 1) * LANES].reshape(
                nz // ny, ny, 2, SUB, LANES
            )
            for c in range(2):
                for g in range(ny):
                    parts[c, s, g, first + i] = (
                        piece[:, g, c].reshape(nz // ny * SUB, LANES).astype(BF16)
                    )

    hidden_t = hidden.T
    for i in range(2):
        emit(3, dot(hidden_t, grad_b[:, i * 256 : i * 256 + 256]), 2 * i)
    pl.semaphore_wait(barrier, n_dp - 1 + n_rep - 1)
    core_copy(3).start()

    loads["wo"].wait()
    wob[...] = wo[...].astype(BF16)
    dhid = dot(grad_b, wob[...], NT).astype(BF16).astype(F32)
    dproj[:, :D] = (dhid * unit_m * slope[:, :D]).astype(BF16)
    dmix = norm_back(dhid * gate[...], unit_m, scale_m).astype(BF16)

    normed_t = normed.T

    def in_part(s):
        for i in range(2):
            n = s * D + i * 256
            emit(s, dot(normed_t, dproj[:, n : n + 256]), 2 * i)
        core_copy(s).start()

    in_part(0)
    core_step(3)

    for blk in range(2):
        top = blk * TILE
        for p in range(HEADS // 2):
            lane = p * LANES
            kk = key[top : top + TILE, lane : lane + LANES]
            qq = qry[top : top + TILE, lane : lane + LANES]
            dq, dk = [], []
            for h in (2 * p, 2 * p + 1):
                dm = dmix[top : top + TILE, h * LANES : (h + 1) * LANES]
                vh = val[top : top + TILE, h * LANES : (h + 1) * LANES]
                w = wts[blk * HEADS + h]
                dw = dot(dm, vh, NT).astype(BF16).astype(F32)
                dv = dot(w, dm, TN).astype(BF16).astype(F32)
                at = D + h * LANES
                dproj[top : top + TILE, at : at + LANES] = (
                    dv * slope[top : top + TILE, at : at + LANES]
                ).astype(BF16)
                ds = (dw * wslope[blk * HEADS + h]).astype(BF16)
                dq.append(dot(ds, kk))
                dk.append(dot(ds, qq, TN))
            for at, pieces in ((2 * D + lane, dq), (2 * D + 256 + lane, dk)):
                both = jnp.where(low, pieces[0], pieces[1]).astype(BF16).astype(F32)
                dproj[top : top + TILE, at : at + LANES] = (
                    both * slope[top : top + TILE, at : at + LANES]
                ).astype(BF16)

    core_step(0)
    in_part(1)
    in_part(2)
    one_step(3)
    core_step(1)

    dnormed = dot(dproj[...], wib[...], NT).astype(BF16).astype(F32)
    grad = norm_back(dnormed, unit, scale) + grad_live
    grad = jnp.where(live, grad, 0.0)
    core_step(2)
    one_step(0)

    to_target = ((tg_row == pair) & (lanes >= 1)).astype(F32).astype(BF16)
    from_slot = at_slot.astype(F32).astype(BF16)
    moves = dot(to_target, from_slot, NT)
    moves = jnp.where(lax.rem(cols, CAP) == lax.rem(row2, CAP), moves, 0.0)
    moved = dot(moves.astype(BF16), grad[TILE:].astype(BF16))
    for i in range(D // LANES):
        spread[pl.ds(i, TILE, stride=D // LANES), :] = moved[:, i * LANES : (i + 1) * LANES]
    send[...] = spread[...].reshape(send.shape).astype(BF16)

    def packed_copy(t):
        return remote(send.at[t], got.at[me], pk_s, pk_r, t, rep)

    @pl.loop(1, n_dp)
    def _(k):
        packed_copy(lax.rem(me + k, n_dp)).start()

    got[me] = send[me]
    home[:TILE] = grad[:TILE]

    two_step(3)
    one_step(1)
    two_step(0)
    one_step(2)
    two_step(1)
    two_step(2)

    nj = nz // ny
    mine = lax.div(z, ny)

    def z_copy(j):
        return remote(
            z_out.at[j], z_in.at[z], z_s, z_r, (j * ny + b) * 2 + core, rep
        )

    @pl.loop(1, nj)
    def _(k):
        z_copy(lax.rem(mine + k, nj)).start()

    @pl.when(jnp.logical_not(holder))
    def _():
        z_copy(mine).start()

    def fin_copy(r):
        return remote(fin_out, fin_in.at[a], f_s.at[r], f_r, me, r)

    @pl.when(holder)
    def _():
        z_in[z] = z_out[mine]
        wait_all(z_in, nz - 1, z_r)
        fin_out[...] = jnp.sum(z_in[...].astype(F32), axis=0).astype(BF16)

        @pl.loop(1, n_rep)
        def _(k):
            fin_copy(lax.rem(rep + k, n_rep)).start()

        fin_in[a] = fin_out[...]

    wait_all(got, n_dp - 1, pk_r)
    spread[...] = got[...].astype(F32).reshape(spread.shape)
    for i in range(D // LANES):
        packed[:, i * LANES : (i + 1) * LANES] = spread[
            pl.ds(i, packed.shape[0], stride=D // LANES), :
        ]

    @pl.when(holder)
    def _():
        wait_all(fin_in, nx - 1, f_r)

    @pl.when(jnp.logical_not(holder))
    def _():
        wait_all(fin_in, nx, f_r)

    for s in range(4):
        for i in range(nx):
            piece = fin_in[i, s].astype(F32)
            if s < 3:
                at = s * D + i * LANES
                grad_in[:, at : at + LANES] = piece
            else:
                grad_out[:, i * LANES : (i + 1) * LANES] = piece

    for s in range(4):
        core_copy(s).wait_send()
        for _, copy in one_copies(s):
            copy(line(s, True)[0]).wait_send()
        for _, copy in two_copies(s):
            copy(line(s, False)[0]).wait_send()
    wait_all(send, n_dp - 1, pk_s)

    @pl.when(holder)
    def _():
        wait_all(z_out, nj - 1, z_s)

        @pl.loop(1, n_rep)
        def _(k):
            fin_copy(lax.rem(rep + k, n_rep)).wait_send()

    @pl.when(jnp.logical_not(holder))
    def _():
        wait_all(z_out, nj, z_s)


def on_device(n_dp, nx, ny, *args):
    nz = n_dp // 2
    deep = nz // ny * SUB
    rows = args[0].shape[0]
    users = args[4].shape
    dma = pltpu.SemaphoreType.DMA
    any_spec = pl.BlockSpec(memory_space=pl.ANY)
    vmem = pl.BlockSpec(memory_space=pltpu.VMEM)
    return pl.pallas_call(
        functools.partial(fused_kernel, n_dp, nx, ny),
        out_shape=(
            jax.ShapeDtypeStruct((rows, D), F32),
            jax.ShapeDtypeStruct((n_dp * CAP, D), F32),
            jax.ShapeDtypeStruct((SUB, F1), F32),
            jax.ShapeDtypeStruct((SUB, D), F32),
        ),
        in_specs=[any_spec] * 7,
        out_specs=(vmem,) * 4,
        scratch_shapes=[
            pltpu.VMEM((rows, D), BF16),
            pltpu.VMEM((rows, D), BF16),
            pltpu.VMEM((D, F1), F32),
            pltpu.VMEM((D, D), F32),
            pltpu.VMEM(users, jnp.int32),
            pltpu.VMEM(users, jnp.int32),
            pltpu.VMEM(users, jnp.int32),
            pltpu.VMEM((D, F1), BF16),
            pltpu.VMEM((D, D), BF16),
            pltpu.VMEM((rows, F1), F32),
            pltpu.VMEM((rows, D), F32),
            pltpu.VMEM((rows, D), BF16),
            pltpu.VMEM((rows, 256), BF16),
            pltpu.VMEM((rows, 256), BF16),
            pltpu.VMEM((2 * HEADS, TILE, TILE), BF16),
            pltpu.VMEM((2 * HEADS, TILE, TILE), F32),
            pltpu.VMEM((rows, D), F32),
            pltpu.VMEM((rows, F1), BF16),
            pltpu.VMEM((TILE * D // LANES, LANES), F32),
            pltpu.VMEM((n_dp, SUB, LANES), BF16),
            pltpu.VMEM((n_dp, SUB, LANES), BF16),
            pltpu.VMEM((2, 4, ny, nx, deep, LANES), BF16),
            pltpu.VMEM((4, ny, nx, deep, LANES), BF16),
            pltpu.VMEM((4, ny, nx, deep, LANES), BF16),
            pltpu.VMEM((4, nx, ny, deep, LANES), BF16),
            pltpu.VMEM((4, nx, deep, LANES), BF16),
            pltpu.VMEM((4, nx, deep, LANES), BF16),
            pltpu.VMEM((nz // ny, 4, SUB, LANES), BF16),
            pltpu.VMEM((nz, 4, SUB, LANES), BF16),
            pltpu.VMEM((4, SUB, LANES), BF16),
            pltpu.VMEM((nx, 4, SUB, LANES), BF16),
            dma((9,)),
            dma, dma,
            dma((4,)), dma((4,)),
            dma((4, nx)), dma((4, nx)),
            dma((4, nx)), dma((4, nx)),
            dma, dma,
            dma((nx * ny,)), dma,
        ],
        compiler_params=pltpu.CompilerParams(
            collective_id=0, has_side_effects=True, vmem_limit_bytes=56 * 2**20
        ),
        name="fused",
    )(*args)


def solution(mesh):
    in_specs = (
        P(("dp", "replica"), None),
        P(("dp", "replica"), None),
        P(),
        P(),
        P(None, "replica", None),
        P(None, "replica", None),
        P(None, "replica", None),
    )
    out_specs = (
        P(("dp", "replica"), None),
        P(("dp", "replica"), None),
        P("dp", None),
        P("dp", None),
    )
    return jax.shard_map(
        functools.partial(on_device, mesh.shape["dp"], 4, mesh.shape["replica"] // 4),
        mesh=mesh,
        in_specs=in_specs,
        out_specs=out_specs,
        check_vma=False,
    )
```

time: 80.9 us -> 76.5 us (0.946)
  the two profiles are of different devices: /device:TPU:4 before, /device:TPU:32 now
where the time goes in v2:
time: 76.5 us; the launch traced here: 76.2 us
  Pallas kernels  69.2 us (90%)
  local copies, waits for them, and re-layouts  6.28 us (8%)
    pallas_call x1, Pallas kernels, on_device(): pl.pallas_call(functools.partial(fused_kernel, n_dp, nx, ny), out_shape=(...  69.2 us
    unnamed x4, local copies, waits for them, and re-layouts  6.28 us

profile of v2, /device:TPU:32, one launch (start us, length us, event | category | flops | bytes accessed | tf_op | source)
XLA Modules:
  0.0 76.2 jit_solution(1023061942410688175)
XLA Ops:
  0.6 69.2 %fused.1 = (f32[256,512]{1,0:T(8,128)}, f32[128,512]{1,0:T(8,128)}, f32[8,1536]{1,0:T(8,128)}, f32[8,512]{1,0:T(8,128)}) custom-call(bf16[256,512]{1,0:T(8,128)(2,1)} %ev_h.1, bf16[256,512]{1,0:T(8,128)(2,1)} %og_h.1, f32[512,1536]{1,0:T(8,128)} %wi_h.1, f32[512,512]{1,0:T(8,128)} %wo_h.1, s32[64,1,65]{2,1,0:T(1,128)} %ln_h.1, s32[64,1,65]{2,1,0:T(1,128)} %of_h.1, ...), custom_call_target="tpu_custom_call" | custom-call | tf_op jit(solution)/shard_map/fused/pallas_call | solution.py:418
  69.9 1.9 %copy.15 = f32[256,512]{1,0:T(8,128)} copy(f32[256,512]{1,0:T(8,128)} %get-tuple-element.8) | data formatting | bytes 1048576
  71.7 1.7 %copy.16 = f32[128,512]{1,0:T(8,128)} copy(f32[128,512]{1,0:T(8,128)} %get-tuple-element.9) | data formatting | bytes 524288
  73.4 1.4 %copy.17 = f32[8,1536]{1,0:T(8,128)} copy(f32[8,1536]{1,0:T(8,128)} %get-tuple-element.10) | data formatting | bytes 98304
  74.8 1.3 %copy.18 = f32[8,512]{1,0:T(8,128)} copy(f32[8,512]{1,0:T(8,128)} %get-tuple-element.11) | data formatting | bytes 32768

commit v3 on v2

--- a/solution.py
+++ b/solution.py
@@ -78,10 +78,15 @@
 
     barrier = pltpu.get_barrier_semaphore()
 
-    @pl.loop(1, n_dp)
-    def _(k):
+    def farthest(i, count):
+        step = lax.div(i + 1, 2)
+        return count // 2 + step * (2 * lax.rem(i + 1, 2) - 1)
+
+    @pl.loop(0, n_dp - 1)
+    def _(i):
+        peer = lax.rem(me + farthest(i, n_dp), n_dp)
         pl.semaphore_signal(
-            barrier, inc=1, device_id=(lax.rem(me + k, n_dp), rep), device_id_type=MESH
+            barrier, inc=1, device_id=(peer, rep), device_id_type=MESH
         )
 
     @pl.loop(1, n_rep)
@@ -165,8 +170,6 @@
     low = lax.broadcasted_iota(jnp.int32, (TILE, LANES), 1) < 64
     zero_b = jnp.zeros((TILE, LANES), BF16)
     pair = lax.div(rows, CAP)
-
-    home[TILE:] = jnp.zeros((TILE, D), F32)
 
     loads["ev"].wait()
     unit, scale = row_norm(ev[...].astype(F32))
@@ -247,8 +250,6 @@
     hidden_t = hidden.T
     for i in range(2):
         emit(3, dot(hidden_t, grad_b[:, i * 256 : i * 256 + 256]), 2 * i)
-    pl.semaphore_wait(barrier, n_dp - 1 + n_rep - 1)
-    core_copy(3).start()
 
     loads["wo"].wait()
     wob[...] = wo[...].astype(BF16)
@@ -262,10 +263,8 @@
         for i in range(2):
             n = s * D + i * 256
             emit(s, dot(normed_t, dproj[:, n : n + 256]), 2 * i)
-        core_copy(s).start()
 
     in_part(0)
-    core_step(3)
 
     for blk in range(2):
         top = blk * TILE
@@ -293,17 +292,12 @@
                     both * slope[top : top + TILE, at : at + LANES]
                 ).astype(BF16)
 
-    core_step(0)
     in_part(1)
     in_part(2)
-    one_step(3)
-    core_step(1)
 
     dnormed = dot(dproj[...], wib[...], NT).astype(BF16).astype(F32)
     grad = norm_back(dnormed, unit, scale) + grad_live
     grad = jnp.where(live, grad, 0.0)
-    core_step(2)
-    one_step(0)
 
     to_target = ((tg_row == pair) & (lanes >= 1)).astype(F32).astype(BF16)
     from_slot = at_slot.astype(F32).astype(BF16)
@@ -314,16 +308,26 @@
         spread[pl.ds(i, TILE, stride=D // LANES), :] = moved[:, i * LANES : (i + 1) * LANES]
     send[...] = spread[...].reshape(send.shape).astype(BF16)
 
+    pl.semaphore_wait(barrier, n_dp - 1 + n_rep - 1)
+    for s in (3, 0, 1, 2):
+        core_copy(s).start()
+
     def packed_copy(t):
         return remote(send.at[t], got.at[me], pk_s, pk_r, t, rep)
 
-    @pl.loop(1, n_dp)
-    def _(k):
-        packed_copy(lax.rem(me + k, n_dp)).start()
+    @pl.loop(0, n_dp - 1)
+    def _(i):
+        packed_copy(lax.rem(me + farthest(i, n_dp), n_dp)).start()
 
     got[me] = send[me]
-    home[:TILE] = grad[:TILE]
-
+    home[...] = grad[:TILE]
+
+    core_step(3)
+    core_step(0)
+    core_step(1)
+    one_step(3)
+    core_step(2)
+    one_step(0)
     two_step(3)
     one_step(1)
     two_step(0)
@@ -339,9 +343,9 @@
             z_out.at[j], z_in.at[z], z_s, z_r, (j * ny + b) * 2 + core, rep
         )
 
-    @pl.loop(1, nj)
-    def _(k):
-        z_copy(lax.rem(mine + k, nj)).start()
+    @pl.loop(0, nj - 1)
+    def _(i):
+        z_copy(lax.rem(mine + farthest(i, nj), nj)).start()
 
     @pl.when(jnp.logical_not(holder))
     def _():
@@ -407,18 +411,66 @@
         wait_all(z_out, nj, z_s)
 
 
+def place_kernel(*refs):
+    count = (len(refs) - 3) // 3
+    sources, targets, held = refs[:count], refs[count : 2 * count], refs[2 * count : -3]
+    zero, inward, outward = refs[-3:]
+    top = sources[0].shape[0]
+    here = [
+        pltpu.make_async_copy(sources[i], held[i], inward.at[i]) for i in range(count)
+    ]
+    there = [
+        pltpu.make_async_copy(
+            held[i], targets[i].at[pl.ds(0, top)] if i == 0 else targets[i], outward.at[i]
+        )
+        for i in range(count)
+    ]
+    for copy in here:
+        copy.start()
+    zero[...] = jnp.zeros_like(zero)
+    rest = pltpu.make_async_copy(
+        zero, targets[0].at[pl.ds(top, zero.shape[0])], outward.at[count]
+    )
+    rest.start()
+    for i in range(count):
+        here[i].wait()
+        there[i].start()
+    for copy in there:
+        copy.wait()
+    rest.wait()
+
+
+def place(home_rows, *results):
+    top = results[0].shape[0]
+    hbm = pl.BlockSpec(memory_space=pltpu.HBM)
+    return pl.pallas_call(
+        place_kernel,
+        out_shape=(jax.ShapeDtypeStruct((home_rows, D), F32),)
+        + tuple(jax.ShapeDtypeStruct(v.shape, v.dtype) for v in results[1:]),
+        in_specs=[hbm] * 4,
+        out_specs=(hbm,) * 4,
+        scratch_shapes=[pltpu.VMEM(v.shape, v.dtype) for v in results]
+        + [
+            pltpu.VMEM((home_rows - top, D), F32),
+            pltpu.SemaphoreType.DMA((4,)),
+            pltpu.SemaphoreType.DMA((5,)),
+        ],
+        name="place",
+    )(*results)
+
+
 def on_device(n_dp, nx, ny, *args):
     nz = n_dp // 2
     deep = nz // ny * SUB
     rows = args[0].shape[0]
     users = args[4].shape
     dma = pltpu.SemaphoreType.DMA
-    any_spec = pl.BlockSpec(memory_space=pl.ANY)
+    any_spec = pl.BlockSpec(memory_space=pltpu.HBM)
     vmem = pl.BlockSpec(memory_space=pltpu.VMEM)
-    return pl.pallas_call(
+    results = pl.pallas_call(
         functools.partial(fused_kernel, n_dp, nx, ny),
         out_shape=(
-            jax.ShapeDtypeStruct((rows, D), F32),
+            jax.ShapeDtypeStruct((TILE, D), F32),
             jax.ShapeDtypeStruct((n_dp * CAP, D), F32),
             jax.ShapeDtypeStruct((SUB, F1), F32),
             jax.ShapeDtypeStruct((SUB, D), F32),
@@ -466,10 +518,11 @@
             dma((nx * ny,)), dma,
         ],
         compiler_params=pltpu.CompilerParams(
-            collective_id=0, has_side_effects=True, vmem_limit_bytes=56 * 2**20
+            collective_id=0, has_side_effects=True, vmem_limit_bytes=58 * 2**20
         ),
         name="fused",
     )(*args)
+    return place(rows, *results)
 
 
 def solution(mesh):

time: 76.5 us -> 64.2 us (0.84)
  the two profiles are of different devices: /device:TPU:32 before, /device:TPU:64 now
where the time goes in v3:
time: 64.2 us; the launch traced here: 64.1 us
  Pallas kernels  63.4 us (99%)
    pallas_call x1, Pallas kernels, on_device(): pl.pallas_call(functools.partial(fused_kernel, n_dp, nx, ny), out_shape=(...  61.5 us
    pallas_call x1, Pallas kernels, place(): pl.pallas_call(place_kernel, out_shape=(jax.ShapeDtypeStruct((home_rows,...  1.92 us

profile of v3, /device:TPU:64, one launch (start us, length us, event | category | flops | bytes accessed | tf_op | source)
XLA Modules:
  0.0 64.1 jit_solution(4312371716527214166)
XLA Ops:
  0.6 61.5 %fused.1 = (f32[128,512]{1,0:T(8,128)}, f32[128,512]{1,0:T(8,128)}, f32[8,1536]{1,0:T(8,128)}, f32[8,512]{1,0:T(8,128)}) custom-call(bf16[256,512]{1,0:T(8,128)(2,1)} %ev_h.1, bf16[256,512]{1,0:T(8,128)(2,1)} %og_h.1, f32[512,1536]{1,0:T(8,128)} %wi_h.1, f32[512,512]{1,0:T(8,128)} %wo_h.1, s32[64,1,65]{2,1,0:T(1,128)} %ln_h.1, s32[64,1,65]{2,1,0:T(1,128)} %of_h.1, ...), custom_call_target="tpu_custom_call" | custom-call | tf_op jit(solution)/shard_map/fused/pallas_call | solution.py:470
  62.2 1.9 %place.1 = (f32[256,512]{1,0:T(8,128)}, f32[128,512]{1,0:T(8,128)}, f32[8,1536]{1,0:T(8,128)}, f32[8,512]{1,0:T(8,128)}) custom-call(f32[128,512]{1,0:T(8,128)} %get-tuple-element.8.refs_0_, f32[128,512]{1,0:T(8,128)} %get-tuple-element.9.refs_1_, f32[8,1536]{1,0:T(8,128)} %get-tuple-element.10.refs_2_, f32[8,512]{1,0:T(8,128)} %get-tuple-element.11.refs_3_), custom_call_target="tpu_custom_call" | custom-call | tf_op jit(solution)/shard_map/place/pallas_call | solution.py:446

commit v4 on v3

--- a/solution.py
+++ b/solution.py
@@ -48,7 +48,7 @@
     n_dp, nx, ny, ev_h, og_h, wi_h, wo_h, ln_h, of_h, tg_h, home, packed, grad_in, grad_out,
     ev, og, wi, wo, ln, of, tg, wib, wob, slope, gate, val, qry, key, wts, wslope, mixed,
     dproj, spread, send, got, parts, core_in, chip, one_in, mid, two_in, z_out, z_in,
-    fin_out, fin_in, ld, pk_s, pk_r, c_s, c_r, o_s, o_r, t_s, t_r, z_s, z_r, f_s, f_r,
+    fin_out, fin_in, ld, pk_s, pk_r, c_s, c_r, o_s, o_r, t_s, t_r, z_s, z_r, f_s, f_r, far_sem,
 ):
     me = lax.axis_index("dp")
     rep = lax.axis_index("replica")
@@ -82,12 +82,15 @@
         step = lax.div(i + 1, 2)
         return count // 2 + step * (2 * lax.rem(i + 1, 2) - 1)
 
-    @pl.loop(0, n_dp - 1)
+    jump = n_dp // 4
+
+    @pl.loop(0, jump + 1)
     def _(i):
-        peer = lax.rem(me + farthest(i, n_dp), n_dp)
-        pl.semaphore_signal(
-            barrier, inc=1, device_id=(peer, rep), device_id_type=MESH
-        )
+        for away in (jump + 1 - i, n_dp - jump - 1 + i):
+            pl.semaphore_signal(
+                barrier, inc=1, device_id=(lax.rem(me + away, n_dp), rep),
+                device_id_type=MESH,
+            )
 
     @pl.loop(1, n_rep)
     def _(k):
@@ -250,6 +253,13 @@
     hidden_t = hidden.T
     for i in range(2):
         emit(3, dot(hidden_t, grad_b[:, i * 256 : i * 256 + 256]), 2 * i)
+    pl.semaphore_wait(barrier, 2 * (jump + 1) + n_rep - 1)
+    for away in (jump, n_dp - jump):
+        pl.semaphore_signal(
+            far_sem, inc=1, device_id=(lax.rem(me + away, n_dp), rep), device_id_type=MESH
+        )
+
+    core_copy(3).start()
 
     loads["wo"].wait()
     wob[...] = wo[...].astype(BF16)
@@ -263,6 +273,7 @@
         for i in range(2):
             n = s * D + i * 256
             emit(s, dot(normed_t, dproj[:, n : n + 256]), 2 * i)
+        core_copy(s).start()
 
     in_part(0)
 
@@ -292,6 +303,8 @@
                     both * slope[top : top + TILE, at : at + LANES]
                 ).astype(BF16)
 
+    core_step(3)
+    core_step(0)
     in_part(1)
     in_part(2)
 
@@ -308,12 +321,13 @@
         spread[pl.ds(i, TILE, stride=D // LANES), :] = moved[:, i * LANES : (i + 1) * LANES]
     send[...] = spread[...].reshape(send.shape).astype(BF16)
 
-    pl.semaphore_wait(barrier, n_dp - 1 + n_rep - 1)
-    for s in (3, 0, 1, 2):
-        core_copy(s).start()
-
     def packed_copy(t):
         return remote(send.at[t], got.at[me], pk_s, pk_r, t, rep)
+
+    core_step(1)
+    core_step(2)
+
+    pl.semaphore_wait(far_sem, 2)
 
     @pl.loop(0, n_dp - 1)
     def _(i):
@@ -322,11 +336,7 @@
     got[me] = send[me]
     home[...] = grad[:TILE]
 
-    core_step(3)
-    core_step(0)
-    core_step(1)
     one_step(3)
-    core_step(2)
     one_step(0)
     two_step(3)
     one_step(1)
@@ -516,6 +526,7 @@
             dma((4, nx)), dma((4, nx)),
             dma, dma,
             dma((nx * ny,)), dma,
+            pltpu.SemaphoreType.REGULAR,
         ],
         compiler_params=pltpu.CompilerParams(
             collective_id=0, has_side_effects=True, vmem_limit_bytes=58 * 2**20

time: 64.2 us -> 62.6 us (0.975)
  Pallas kernels: 63.4 us -> 61.8 us
    pallas_call x1, Pallas kernels: 61.5 us -> 59.8 us  [on_device(): pl.pallas_call(functools.partial(fused_kernel, n_dp, nx, ny), out_shape=(...]
where the time goes in v4:
time: 62.6 us; the launch traced here: 62.4 us
  Pallas kernels  61.8 us (99%)
  between operations  0.64 us (1%)
    pallas_call x1, Pallas kernels, on_device(): pl.pallas_call(functools.partial(fused_kernel, n_dp, nx, ny), out_shape=(...  59.8 us
    pallas_call x1, Pallas kernels, place(): pl.pallas_call(place_kernel, out_shape=(jax.ShapeDtypeStruct((home_rows,...  1.92 us

profile of v4, /device:TPU:64, one launch (start us, length us, event | category | flops | bytes accessed | tf_op | source)
XLA Modules:
  0.0 62.4 jit_solution(573698832423099162)
XLA Ops:
  0.6 59.8 %fused.1 = (f32[128,512]{1,0:T(8,128)}, f32[128,512]{1,0:T(8,128)}, f32[8,1536]{1,0:T(8,128)}, f32[8,512]{1,0:T(8,128)}) custom-call(bf16[256,512]{1,0:T(8,128)(2,1)} %ev_h.1, bf16[256,512]{1,0:T(8,128)(2,1)} %og_h.1, f32[512,1536]{1,0:T(8,128)} %wi_h.1, f32[512,512]{1,0:T(8,128)} %wo_h.1, s32[64,1,65]{2,1,0:T(1,128)} %ln_h.1, s32[64,1,65]{2,1,0:T(1,128)} %of_h.1, ...), custom_call_target="tpu_custom_call" | custom-call | tf_op jit(solution)/shard_map/fused/pallas_call | solution.py:480
  60.5 1.9 %place.1 = (f32[256,512]{1,0:T(8,128)}, f32[128,512]{1,0:T(8,128)}, f32[8,1536]{1,0:T(8,128)}, f32[8,512]{1,0:T(8,128)}) custom-call(f32[128,512]{1,0:T(8,128)} %get-tuple-element.8.refs_0_, f32[128,512]{1,0:T(8,128)} %get-tuple-element.9.refs_1_, f32[8,1536]{1,0:T(8,128)} %get-tuple-element.10.refs_2_, f32[8,512]{1,0:T(8,128)} %get-tuple-element.11.refs_3_), custom_call_target="tpu_custom_call" | custom-call | tf_op jit(solution)/shard_map/place/pallas_call | solution.py:456

commit v5 on v4

--- a/solution.py
+++ b/solution.py
@@ -336,14 +336,9 @@
     got[me] = send[me]
     home[...] = grad[:TILE]
 
-    one_step(3)
-    one_step(0)
-    two_step(3)
-    one_step(1)
-    two_step(0)
-    one_step(2)
-    two_step(1)
-    two_step(2)
+    for step in (one_step, two_step):
+        for s in (3, 0, 1, 2):
+            step(s)
 
     nj = nz // ny
     mine = lax.div(z, ny)

time: 62.6 us -> 63.4 us (1.013)
  Pallas kernels: 61.8 us -> 62.6 us
    pallas_call x1, Pallas kernels: 59.8 us -> 60.7 us  [on_device(): pl.pallas_call(functools.partial(fused_kernel, n_dp, nx, ny), out_shape=(...]
where the time goes in v5:
time: 63.4 us; the launch traced here: 63.3 us
  Pallas kernels  62.6 us (99%)
  between operations  0.64 us (1%)
    pallas_call x1, Pallas kernels, on_device(): pl.pallas_call(functools.partial(fused_kernel, n_dp, nx, ny), out_shape=(...  60.7 us
    pallas_call x1, Pallas kernels, place(): pl.pallas_call(place_kernel, out_shape=(jax.ShapeDtypeStruct((home_rows,...  1.92 us

profile of v5, /device:TPU:64, one launch (start us, length us, event | category | flops | bytes accessed | tf_op | source)
XLA Modules:
  0.0 63.3 jit_solution(3179816264542978079)
XLA Ops:
  0.6 60.7 %fused.1 = (f32[128,512]{1,0:T(8,128)}, f32[128,512]{1,0:T(8,128)}, f32[8,1536]{1,0:T(8,128)}, f32[8,512]{1,0:T(8,128)}) custom-call(bf16[256,512]{1,0:T(8,128)(2,1)} %ev_h.1, bf16[256,512]{1,0:T(8,128)(2,1)} %og_h.1, f32[512,1536]{1,0:T(8,128)} %wi_h.1, f32[512,512]{1,0:T(8,128)} %wo_h.1, s32[64,1,65]{2,1,0:T(1,128)} %ln_h.1, s32[64,1,65]{2,1,0:T(1,128)} %of_h.1, ...), custom_call_target="tpu_custom_call" | custom-call | tf_op jit(solution)/shard_map/fused/pallas_call | solution.py:475
  61.3 1.9 %place.1 = (f32[256,512]{1,0:T(8,128)}, f32[128,512]{1,0:T(8,128)}, f32[8,1536]{1,0:T(8,128)}, f32[8,512]{1,0:T(8,128)}) custom-call(f32[128,512]{1,0:T(8,128)} %get-tuple-element.8.refs_0_, f32[128,512]{1,0:T(8,128)} %get-tuple-element.9.refs_1_, f32[8,1536]{1,0:T(8,128)} %get-tuple-element.10.refs_2_, f32[8,512]{1,0:T(8,128)} %get-tuple-element.11.refs_3_), custom_call_target="tpu_custom_call" | custom-call | tf_op jit(solution)/shard_map/place/pallas_call | solution.py:451
